TPU v7x, 512 devices: a whole 4x4x16 slice. The times are simulated.
512 devices in a mesh: gx: 32 (over z_hi, x, core), gy: 16 (over y, z_lo).
Axes of the slice: x: 4, y: 4, z: 16 (z_hi: 4, z_lo: 4; z = z_hi * 4 + z_lo), core: 2. Of those that a mesh axis runs over, the one named last changes fastest.
Arguments:
- feats: bfloat16 [32, 16, 2, 128, 512], P('gx', 'gy'), may hold values from -12 to 12
- w_query: bfloat16 [512, 512], replicated, may hold values from -1 to 1
- w_key: bfloat16 [512, 512], replicated, may hold values from -1 to 1
- w_value: bfloat16 [512, 512], replicated, may hold values from -0.25 to 0.25
- out_grad: bfloat16 [32, 16, 2, 128, 512], P('gx', 'gy'), may hold values from -6 to 6
- patch_count: int32 [32, 16], P('gx', 'gy'), may hold values from 1 to 2
- point_count: int32 [32, 16, 2], P('gx', 'gy'), may hold values from 32 to 128
- neighbours: int32 [32, 16, 2, 3], P('gx', 'gy'), may hold values from 0 to 9, as said below
- neighbour_points: int32 [32, 16, 2, 3], P('gx', 'gy'), may hold values from 32 to 128, as said below
Outputs:
- mixed: bfloat16 [32, 16, 2, 128, 512], P('gx', 'gy')
- feat_grad: bfloat16 [32, 16, 2, 128, 512], P('gx', 'gy')
- grad_query: bfloat16 [512, 512], replicated
- grad_key: bfloat16 [512, 512], replicated
- grad_value: bfloat16 [512, 512], replicated
Inputs may be any that keep to these rules, and one draw needn't show every extreme that they name: `neighbour_points`: equal to point_count of the patch that the same entry of neighbours names.
All inputs are finite; a program needn't handle non-finite values.
Results may differ from a plain program's by a relative error of at most 0.015.
Values may be sent and summed in bfloat16 or wider, within the bound.
A program may use at most 64 MiB of HBM per device.

v0:
```python
import jax
import jax.numpy as jnp
from jax import lax
from jax.sharding import PartitionSpec as P

HEADS = 8


def with_halo(x, sides, width):
    for axis, dim in sides:
        peers, length = (lax.axis_size(axis), x.shape[dim])
        up = [(i, (i + 1) % peers) for i in range(peers - 1)]
        down = [(j, i) for i, j in up]
        last = lax.slice_in_dim(x, length - width, length, axis=dim)
        initial = lax.slice_in_dim(x, 0, width, axis=dim)
        before = lax.ppermute(last, axis, up)
        after = lax.ppermute(initial, axis, down)
        x = jnp.concatenate([before, x, after], axis=dim)
    return x


def passed_along(value, axis, steps):
    count = lax.axis_size(axis)
    initial, last = (max(0, -steps), min(count, count - steps))
    return lax.ppermute(value, axis, [(source, source + steps) for source in range(initial, last)])


def one_slot(items):
    qq, keys, key_valid, live, grads = items
    points, width = qq.shape
    head_dim = width // HEADS
    scale = head_dim ** (-0.5)
    kk = keys[:, :width].reshape(-1, HEADS, head_dim)
    vv = keys[:, width:].reshape(-1, HEADS, head_dim)
    qh = qq.reshape(points, HEADS, head_dim)
    scores = jnp.einsum("qhd,khd->hqk", qh, kk, preferred_element_type=jnp.float32) * scale
    scores = jnp.where(key_valid[None, None, :], scores, -1e30)
    top = jnp.max(scores, axis=-1, keepdims=True)
    expo = jnp.exp(scores - top)
    probs = expo / jnp.sum(expo, axis=-1, keepdims=True)
    probs_b = probs.astype(jnp.bfloat16)
    mixed = jnp.einsum("hqk,khd->qhd", probs_b, vv, preferred_element_type=jnp.float32)
    alive = live[:, None, None]
    out = jnp.where(alive, mixed, 0.0).astype(jnp.bfloat16).reshape(points, width)
    gradh = grads.reshape(points, HEADS, head_dim)
    dout = jnp.where(alive, gradh, jnp.zeros_like(gradh))
    dprob = jnp.einsum("qhd,khd->hqk", dout, vv, preferred_element_type=jnp.float32)
    inner = jnp.sum(probs * dprob, axis=-1, keepdims=True)
    dscore = (probs * (dprob - inner) * scale).astype(jnp.bfloat16)
    dquery = jnp.einsum("hqk,khd->qhd", dscore, kk, preferred_element_type=jnp.float32)
    dquery = dquery.astype(jnp.bfloat16).reshape(points, width)
    dkey = jnp.einsum("hqk,qhd->khd", dscore, qh, preferred_element_type=jnp.float32)
    dval = jnp.einsum("hqk,qhd->khd", probs_b, dout, preferred_element_type=jnp.float32)
    contrib = jnp.concatenate(
        [dkey.reshape(-1, points, width), dval.reshape(-1, points, width)], axis=-1
    )
    return (out, dquery, contrib)


def attend(query, table, codes, key_len, q_valid, grad_out):
    slots, points, width = query.shape
    keys = table.reshape(-1, points, 2 * width)[codes].reshape(slots, -1, 2 * width)
    key_valid = (jnp.arange(points, dtype=jnp.int32)[None, None, :] < key_len[:, :, None]).reshape(
        slots, -1
    )
    out, dquery, contrib = lax.map(one_slot, (query, keys, key_valid, q_valid, grad_out))
    contrib = contrib.reshape(-1, points * 2 * width)
    onehot = (jnp.arange(5 * slots, dtype=jnp.int32)[:, None] == codes.reshape(1, -1)).astype(
        jnp.float32
    )
    partial_value = jnp.dot(
        onehot, contrib, precision=lax.Precision.HIGHEST, preferred_element_type=jnp.float32
    )
    partial_value = partial_value.astype(jnp.bfloat16).reshape(5, slots, points, 2 * width)
    return (out, dquery, partial_value)


def faces_of(wide):
    return jnp.stack([wide[0, 1], wide[2, 1], wide[1, 0], wide[1, 2]])


def project(rows, weight):
    return jnp.dot(rows, weight, preferred_element_type=jnp.float32).astype(jnp.bfloat16)


def body(
    feats, w_query, w_key, w_value, out_grad, patch_count, point_count, neighbours, neighbour_points
):
    slots, points, width = (feats.shape[2], feats.shape[3], feats.shape[4])
    flat = feats.reshape(-1, width)
    query = project(flat, w_query).reshape(slots, points, width)
    keyval = jnp.concatenate([project(flat, w_key), project(flat, w_value)], axis=-1).reshape(
        slots, points, 2 * width
    )
    wide = with_halo(keyval[None, None], (("gx", 0), ("gy", 1)), 1)
    faces = faces_of(wide)
    table = jnp.concatenate([keyval[None], faces], axis=0)
    codes = jnp.concatenate([jnp.arange(slots, dtype=jnp.int32)[:, None], neighbours[0, 0]], axis=1)
    counts = point_count[0, 0]
    key_len = jnp.concatenate([counts[:, None], neighbour_points[0, 0]], axis=1)
    q_valid = (jnp.arange(slots, dtype=jnp.int32)[:, None] < patch_count[0, 0]) & (
        jnp.arange(points, dtype=jnp.int32)[None, :] < counts[:, None]
    )
    out, dquery, partial_value = attend(query, table, codes, key_len, q_valid, out_grad[0, 0])
    total = partial_value[0].astype(jnp.float32)
    for shift_by, place in ((-1, 1), (1, 2)):
        total = total + passed_along(partial_value[place], "gx", shift_by).astype(jnp.float32)
    for shift_by, place in ((-1, 3), (1, 4)):
        total = total + passed_along(partial_value[place], "gy", shift_by).astype(jnp.float32)
    grads = total.astype(jnp.bfloat16)
    dq = dquery.reshape(-1, width)
    dk = grads[..., :width].reshape(-1, width)
    dv = grads[..., width:].reshape(-1, width)
    back = (((1,), (1,)), ((), ()))
    feat_grad = (
        lax.dot_general(dq, w_query, back, preferred_element_type=jnp.float32)
        + lax.dot_general(dk, w_key, back, preferred_element_type=jnp.float32)
        + lax.dot_general(dv, w_value, back, preferred_element_type=jnp.float32)
    )
    feat_grad = feat_grad.astype(jnp.bfloat16).reshape(feats.shape)
    outer = (((0,), (0,)), ((), ()))
    local_q = lax.dot_general(flat, dq, outer, preferred_element_type=jnp.float32)
    local_k = lax.dot_general(flat, dk, outer, preferred_element_type=jnp.float32)
    local_v = lax.dot_general(flat, dv, outer, preferred_element_type=jnp.float32)
    sum_q, sum_k, sum_v = lax.psum((local_q, local_k, local_v), ("gx", "gy"))
    mixed = out.reshape(feats.shape)
    return (
        mixed,
        feat_grad,
        sum_q.astype(jnp.bfloat16),
        sum_k.astype(jnp.bfloat16),
        sum_v.astype(jnp.bfloat16),
    )


def solution(mesh):
    return jax.shard_map(
        body,
        mesh=mesh,
        in_specs=(
            P("gx", "gy", None, None, None),
            P(),
            P(),
            P(),
            P("gx", "gy", None, None, None),
            P("gx", "gy"),
            P("gx", "gy", None),
            P("gx", "gy", None, None),
            P("gx", "gy", None, None),
        ),
        out_specs=(P("gx", "gy", None, None, None), P("gx", "gy", None, None, None), P(), P(), P()),
        check_vma=False,
    )
```

profile of v0, /device:TPU:8, one launch (start us, length us, event | category | flops | bytes accessed | tf_op | source)
XLA Modules:
  0.0 444.8 jit_solution(17124175754200817036)
XLA Ops:
  5.0 3.1 collective-permute-start
  10.9 3.8 collective-permute-start.2
  15.7 4.7 %collective-permute-start.3 = (bf16[3,1,2,128,1024]{4,3,2,1,0:T(8,128)(2,1)}, bf16[3,1,2,128,1024]{4,3,2,1,0:T(8,128)(2,1)S(1)}, u32[]{:S(2)}, u32[]{:S(2)}) collective-permute-start(bf16[3,1,2,128,1024]{4,3,2,1,0:T(8,128)(2,1)} %pad_maximum_fusion), channel_id=1, source_target_pairs={{1,0},{2,1},{3,2},{4,3},{5,4},{6,5},{7,6},{8,7},{9,8},{10,9},{11,1... | collective-permute-start | bytes 4718600 | tf_op jit(solution)/shard_map/ppermute | solution.py:17
  24.1 39.3 %collective-permute-done.2 = bf16[3,1,2,128,1024]{4,3,2,1,0:T(8,128)(2,1)} collective-permute-done((bf16[3,1,2,128,1024]{4,3,2,1,0:T(8,128)(2,1)}, bf16[3,1,2,128,1024]{4,3,2,1,0:T(8,128)(2,1)}, u32[]{:S(2)}, u32[]{:S(2)}) %collective-permute-start.2) | collective-permute-done | bytes 1572896 | tf_op jit(solution)/shard_map/ppermute | solution.py:16
  65.3 22.7 %collective-permute-done.3 = bf16[3,1,2,128,1024]{4,3,2,1,0:T(8,128)(2,1)S(1)} collective-permute-done((bf16[3,1,2,128,1024]{4,3,2,1,0:T(8,128)(2,1)}, bf16[3,1,2,128,1024]{4,3,2,1,0:T(8,128)(2,1)S(1)}, u32[]{:S(2)}, u32[]{:S(2)}) %collective-permute-start.3) | collective-permute-done | bytes 1572896 | tf_op jit(solution)/shard_map/ppermute | solution.py:17
  88.8 3.8 gather_fusion
  92.6 81.0 %while.14 = (s32[]{:T(128)}, bf16[2,128,512]{2,1,0:T(8,128)(2,1)}, bf16[2,128,512]{2,1,0:T(8,128)(2,1)}, f32[2,4,128,1024]{3,2,1,0:T(8,128)}, pred[2,128]{1,0:T(...) while((s32[]{:T(128)}, bf16[2,128,512]{2,1,0:T(8,128)(2,1)}, ...), condition=%wide.region_4.5_spmd, body=%wide.region_0.4_spmd.sunk | while | flops 415043072 | bytes 50373096 | solution.py:66
  99.0 3.9 fusion.108
  102.9 2.8 fusion.110
  105.7 8.5 %fusion.109 = bf16[8,64,128]{2,1,0:T(8,128)(2,1)} fusion(bf16[512,8,64]{0,2,1:T(8,128)(2,1)} %bitcast.165, f32[8,128,512]{2,1,0:T(8,128)S(1)} %fusion.107, f32[8,128,512]{2,1,0:T(8,128)} %get-tuple-element.182, f32[8,128]{1,0:T(8,128)S(1)} %copy-done.16), kind=kOutput, calls=%fused_computation.15.clone.1 | convolution fusion | flops 70845952 | bytes 4853760 | tf_op jit(solution)/shard_map/while/body/eval_jaxpr/hqk,khd->qhd/dot_general | solution.py:50
  114.2 8.8 %fusion.111 = f32[512,8,64]{0,2,1:T(8,128)} fusion(bf16[128,8,64]{0,2,1:T(8,128)(2,1)S(1)} %bitcast.180, f32[8,128,512]{2,1,0:T(8,128)S(1)} %fusion.107, f32[8,128,512]{2,1,0:T(8,128)} %get-tuple-element.182, f32[8,128]{1,0:T(8,128)S(1)} %copy-done.16), kind=kOutput, calls=%fused_computation.12.clone.1 | convolution fusion | flops 70780416 | bytes 5378048 | tf_op jit(solution)/shard_map/while/body/eval_jaxpr/hqk,qhd->khd/dot_general | solution.py:52
  139.5 3.9 fusion.108
  143.4 2.8 fusion.110
  146.2 8.5 %fusion.109 = bf16[8,64,128]{2,1,0:T(8,128)(2,1)} fusion(bf16[512,8,64]{0,2,1:T(8,128)(2,1)} %bitcast.165, f32[8,128,512]{2,1,0:T(8,128)S(1)} %fusion.107, f32[8,128,512]{2,1,0:T(8,128)} %get-tuple-element.182, f32[8,128]{1,0:T(8,128)S(1)} %copy-done.16), kind=kOutput, calls=%fused_computation.15.clone.1 | convolution fusion | flops 70845952 | bytes 4853760 | tf_op jit(solution)/shard_map/while/body/eval_jaxpr/hqk,khd->qhd/dot_general | solution.py:50
  154.7 8.8 %fusion.111 = f32[512,8,64]{0,2,1:T(8,128)} fusion(bf16[128,8,64]{0,2,1:T(8,128)(2,1)S(1)} %bitcast.180, f32[8,128,512]{2,1,0:T(8,128)S(1)} %fusion.107, f32[8,128,512]{2,1,0:T(8,128)} %get-tuple-element.182, f32[8,128]{1,0:T(8,128)S(1)} %copy-done.16), kind=kOutput, calls=%fused_computation.12.clone.1 | convolution fusion | flops 70780416 | bytes 5378048 | tf_op jit(solution)/shard_map/while/body/eval_jaxpr/hqk,qhd->khd/dot_general | solution.py:52
  173.6 4.6 %copy.40 = f32[1,8,128,1024]{3,1,2,0:T(8,128)S(1)} copy(f32[1,8,128,1024]{3,2,1,0:T(8,128)} %bitcast.176) | data formatting | bytes 8388608
  178.3 3.6 convolution_convert_fusion
  184.2 4.7 %collective-permute-start.5 = (bf16[2,128,1024]{2,1,0:T(8,128)(2,1)S(1)}, bf16[2,128,1024]{2,1,0:T(8,128)(2,1)S(1)}, u32[]{:S(2)}, u32[]{:S(2)}) collective-permute-start(bf16[2,128,1024]{2,1,0:T(8,128)(2,1)S(1)} %bitcast.195), channel_id=1, source_target_pairs={{0,16},{16,32},{32,48},{48,64},{64,80},{80,96},{96,112},{112,128},... | collective-permute-start | bytes 1572872 | tf_op jit(solution)/shard_map/ppermute | solution.py:25
  188.9 10.2 %collective-permute-start.6 = (bf16[2,128,1024]{2,1,0:T(8,128)(2,1)S(1)}, bf16[2,128,1024]{2,1,0:T(8,128)(2,1)S(1)}, u32[]{:S(2)}, u32[]{:S(2)}) collective-permute-start(bf16[2,128,1024]{2,1,0:T(8,128)(2,1)S(1)} %bitcast.194), channel_id=1, source_target_pairs={{1,0},{2,1},{3,2},{4,3},{5,4},{6,5},{7,6},{8,7},{9,8},{10,9},{11,1... | collective-permute-start | bytes 1572872 | tf_op jit(solution)/shard_map/ppermute | solution.py:25
  203.1 8.4 %collective-permute-done.6 = bf16[2,128,1024]{2,1,0:T(8,128)(2,1)S(1)} collective-permute-done((bf16[2,128,1024]{2,1,0:T(8,128)(2,1)S(1)}, bf16[2,128,1024]{2,1,0:T(8,128)(2,1)S(1)}, u32[]{:S(2)}, u32[]{:S(2)}) %collective-permute-start.6) | collective-permute-done | bytes 524320 | tf_op jit(solution)/shard_map/ppermute | solution.py:25
  211.5 18.7 %collective-permute-done.7 = bf16[2,128,1024]{2,1,0:T(8,128)(2,1)S(1)} collective-permute-done((bf16[2,128,1024]{2,1,0:T(8,128)(2,1)S(1)}, bf16[2,128,1024]{2,1,0:T(8,128)(2,1)S(1)}, u32[]{:S(2)}, u32[]{:S(2)}) %collective-permute-start.7) | collective-permute-done | bytes 524320 | tf_op jit(solution)/shard_map/ppermute | solution.py:25
  234.6 205.1 %all-reduce.2 = (bf16[512,512]{0,1:T(8,128)(2,1)}, bf16[512,512]{0,1:T(8,128)(2,1)}, bf16[512,512]{0,1:T(8,128)(2,1)S(1)}) all-reduce(f32[512,512]{0,1:T(8,128)S(1)} %convolution_bitcast_fusion.3, f32[512,512]{0,1:T(8,128)S(1)} %convolution_bitcast_fusion.2, ...), channel_id=1, replica_groups=mesh['gx'=32,'gy'=16] {'gx','gy'}, use_global_device_ids=true, to_apply=%region_5.6 | all-reduce | flops 786432 | bytes 4718592 | tf_op jit(solution)/shard_map/psum | solution.py:125
  439.7 2.0 copy.28
  441.8 2.0 copy.29
  (135 shorter events, 58.1 us)
Async XLA Ops:
  0.6 20.7 %copy-start = (bf16[512,512]{1,0:T(8,128)(2,1)S(1)}, bf16[512,512]{1,0:T(8,128)(2,1)}, u32[]{:S(2)}) copy-start(bf16[512,512]{1,0:T(8,128)(2,1)} %param.12) | copy-start | bytes 1572868
  0.6 8.0 %copy-start.13 = (s32[1,1,2]{2,1,0:T(1,128)S(1)}, s32[1,1,2]{2,1,0:T(1,128)}, u32[]{:S(2)}) copy-start(s32[1,1,2]{2,1,0:T(1,128)} %param.17) | copy-start | bytes 28
  0.7 8.1 %copy-start.11 = (s32[1,1,2,3]{3,2,1,0:T(2,128)S(1)}, s32[1,1,2,3]{3,2,1,0:T(2,128)}, u32[]{:S(2)}) copy-start(s32[1,1,2,3]{3,2,1,0:T(2,128)} %param.18) | copy-start | bytes 76
  0.7 8.3 %copy-start.12 = (s32[1,1,2,3]{3,2,1,0:T(2,128)S(1)}, s32[1,1,2,3]{3,2,1,0:T(2,128)}, u32[]{:S(2)}) copy-start(s32[1,1,2,3]{3,2,1,0:T(2,128)} %param.19) | copy-start | bytes 76
  3.6 11.2 %copy-start.10 = (bf16[1,1,2,128,512]{4,3,2,1,0:T(8,128)(2,1)S(1)}, bf16[1,1,2,128,512]{4,3,2,1,0:T(8,128)(2,1)}, u32[]{:S(2)}) copy-start(bf16[1,1,2,128,512]{4,3,2,1,0:T(8,128)(2,1)} %param.15) | copy-start | bytes 786436
  3.7 5.5 %collective-permute-start.1 = (bf16[1,1,2,128,1024]{4,3,2,1,0:T(8,128)(2,1)S(1)}, bf16[1,1,2,128,1024]{4,3,2,1,0:T(8,128)(2,1)S(1)}, u32[]{:S(2)}, u32[]{:S(2)}) collective-permute-start(bf16[1,1,2,128,1024]{4,3,2,1,0:T(8,128)(2,1)S(1)} %bitcast.172), channel_id=1, source_target_pairs={{16,0},{32,16},{48,32},{64,48},{80,64},{96,80},{112,96},{128,112},... | collective-permute-start | bytes 1572872 | tf_op jit(solution)/shard_map/ppermute | solution.py:17
  5.0 4.6 %collective-permute-start = (bf16[1,1,2,128,1024]{4,3,2,1,0:T(8,128)(2,1)S(1)}, bf16[1,1,2,128,1024]{4,3,2,1,0:T(8,128)(2,1)S(1)}, u32[]{:S(2)}, u32[]{:S(2)}) collective-permute-start(bf16[1,1,2,128,1024]{4,3,2,1,0:T(8,128)(2,1)S(1)} %bitcast.173), channel_id=1, source_target_pairs={{0,16},{16,32},{32,48},{48,64},{64,80},{80,96},{96,112},{112,128},... | collective-permute-start | bytes 1572872 | tf_op jit(solution)/shard_map/ppermute | solution.py:16
  9.1 12.3 %copy-start.1 = (bf16[1,1,2,128,512]{4,3,2,1,0:T(8,128)(2,1)S(1)}, bf16[1,1,2,128,512]{4,3,2,1,0:T(8,128)(2,1)}, u32[]{:S(2)}) copy-start(bf16[1,1,2,128,512]{4,3,2,1,0:T(8,128)(2,1)} %param.11) | copy-start | bytes 786436
  10.9 52.5 %collective-permute-start.2 = (bf16[3,1,2,128,1024]{4,3,2,1,0:T(8,128)(2,1)}, bf16[3,1,2,128,1024]{4,3,2,1,0:T(8,128)(2,1)}, u32[]{:S(2)}, u32[]{:S(2)}) collective-permute-start(bf16[3,1,2,128,1024]{4,3,2,1,0:T(8,128)(2,1)} %pad_maximum_fusion), channel_id=1, source_target_pairs={{0,1},{1,2},{2,3},{3,4},{4,5},{5,6},{6,7},{7,8},{8,9},{9,10},{10,1... | collective-permute-start | bytes 4718600 | tf_op jit(solution)/shard_map/ppermute | solution.py:16
  15.7 72.2 %collective-permute-start.3 = (bf16[3,1,2,128,1024]{4,3,2,1,0:T(8,128)(2,1)}, bf16[3,1,2,128,1024]{4,3,2,1,0:T(8,128)(2,1)S(1)}, u32[]{:S(2)}, u32[]{:S(2)}) collective-permute-start(bf16[3,1,2,128,1024]{4,3,2,1,0:T(8,128)(2,1)} %pad_maximum_fusion), channel_id=1, source_target_pairs={{1,0},{2,1},{3,2},{4,3},{5,4},{6,5},{7,6},{8,7},{9,8},{10,9},{11,1... | collective-permute-start | bytes 4718600 | tf_op jit(solution)/shard_map/ppermute | solution.py:17
  102.9 2.8 copy-start.16
  105.7 8.5 %copy-start.3 = (bf16[1,128,512]{1,2,0:T(8,128)(2,1)S(1)}, bf16[1,128,512]{1,2,0:T(8,128)(2,1)}, u32[]{:S(2)}) copy-start(bf16[1,128,512]{1,2,0:T(8,128)(2,1)} %copy.62) | copy-start | bytes 393220 | tf_op jit(solution)/shard_map/while
  128.7 2.0 copy-start.4
  128.7 2.1 copy-start.2
  128.7 2.3 copy-start.7
  143.4 2.8 copy-start.16
  146.2 8.5 %copy-start.3 = (bf16[1,128,512]{1,2,0:T(8,128)(2,1)S(1)}, bf16[1,128,512]{1,2,0:T(8,128)(2,1)}, u32[]{:S(2)}) copy-start(bf16[1,128,512]{1,2,0:T(8,128)(2,1)} %copy.62) | copy-start | bytes 393220 | tf_op jit(solution)/shard_map/while
  169.2 2.1 copy-start.2
  169.2 2.3 copy-start.7
  183.7 18.6 %copy-start.9 = (bf16[2,128,512]{2,1,0:T(8,128)(2,1)S(1)}, bf16[2,128,512]{2,1,0:T(8,128)(2,1)}, u32[]{:S(2)}) copy-start(bf16[2,128,512]{2,1,0:T(8,128)(2,1)} %get-tuple-element.55) | copy-start | bytes 786436
  184.2 18.8 %collective-permute-start.5 = (bf16[2,128,1024]{2,1,0:T(8,128)(2,1)S(1)}, bf16[2,128,1024]{2,1,0:T(8,128)(2,1)S(1)}, u32[]{:S(2)}, u32[]{:S(2)}) collective-permute-start(bf16[2,128,1024]{2,1,0:T(8,128)(2,1)S(1)} %bitcast.195), channel_id=1, source_target_pairs={{0,16},{16,32},{32,48},{48,64},{64,80},{80,96},{96,112},{112,128},... | collective-permute-start | bytes 1572872 | tf_op jit(solution)/shard_map/ppermute | solution.py:25
  188.9 22.5 %collective-permute-start.6 = (bf16[2,128,1024]{2,1,0:T(8,128)(2,1)S(1)}, bf16[2,128,1024]{2,1,0:T(8,128)(2,1)S(1)}, u32[]{:S(2)}, u32[]{:S(2)}) collective-permute-start(bf16[2,128,1024]{2,1,0:T(8,128)(2,1)S(1)} %bitcast.194), channel_id=1, source_target_pairs={{1,0},{2,1},{3,2},{4,3},{5,4},{6,5},{7,6},{8,7},{9,8},{10,9},{11,1... | collective-permute-start | bytes 1572872 | tf_op jit(solution)/shard_map/ppermute | solution.py:25
  199.1 31.1 %collective-permute-start.7 = (bf16[2,128,1024]{2,1,0:T(8,128)(2,1)S(1)}, bf16[2,128,1024]{2,1,0:T(8,128)(2,1)S(1)}, u32[]{:S(2)}, u32[]{:S(2)}) collective-permute-start(bf16[2,128,1024]{2,1,0:T(8,128)(2,1)S(1)} %bitcast.193), channel_id=1, source_target_pairs={{0,1},{1,2},{2,3},{3,4},{4,5},{5,6},{6,7},{7,8},{8,9},{9,10},{10,1... | collective-permute-start | bytes 1572872 | tf_op jit(solution)/shard_map/ppermute | solution.py:25
  201.1 29.1 %collective-permute-start.4 = (bf16[2,128,1024]{2,1,0:T(8,128)(2,1)S(1)}, bf16[2,128,1024]{2,1,0:T(8,128)(2,1)S(1)}, u32[]{:S(2)}, u32[]{:S(2)}) collective-permute-start(bf16[2,128,1024]{2,1,0:T(8,128)(2,1)S(1)} %bitcast.192), channel_id=1, source_target_pairs={{16,0},{32,16},{48,32},{64,48},{80,64},{96,80},{112,96},{128,112},... | collective-permute-start | bytes 1572872 | tf_op jit(solution)/shard_map/ppermute | solution.py:25
  (9 other events, 11.6 us)
where the time goes:
time: 446 us; the launch traced here: 445 us
  blocking collectives  205 us (46%)
  waiting for transfers between devices  89.5 us (20%)
  matrix products  64.1 us (14%)
  local copies, waits for them, and re-layouts  45.5 us (10%)
  starting transfers between devices  31 us (7%)
  other arithmetic  7.84 us (2%)
    psum x1, blocking collectives, body(): sum_q, sum_k, sum_v = lax.psum((local_q, local_k, local_v), ('gx', 'gy'))  205 us
    ppermute x2, waiting for transfers between devices, with_halo(): before = lax.ppermute(last, axis, up)  39.7 us
    ppermute x4, waiting for transfers between devices, passed_along(): lax.ppermute(value, axis, [(source, source + steps) for source in range(i...  27.2 us
    ppermute x2, waiting for transfers between devices, with_halo(): after = lax.ppermute(initial, axis, down)  22.7 us
    ppermute x4, starting transfers between devices, passed_along(): lax.ppermute(value, axis, [(source, source + steps) for source in range(i...  18.1 us
    dot_general x2, matrix products, one_slot(): jnp.einsum('hqk,qhd->khd', dscore, qh, preferred_element_type=jnp.float32)  17.6 us
    dot_general x2, matrix products, one_slot(): jnp.einsum('hqk,khd->qhd', dscore, kk, preferred_element_type=jnp.float32)  17.1 us
    unnamed x32, local copies, waits for them, and re-layouts  16.2 us
  transfers between devices with their start and end apart: 8, of which 5 were waited for; matrix products, arithmetic and copies ran while one was open for 2% of the time, Pallas kernels for 0%

commit v1 on v0

--- a/solution.py
+++ b/solution.py
@@ -122,7 +122,8 @@
     local_q = lax.dot_general(flat, dq, outer, preferred_element_type=jnp.float32)
     local_k = lax.dot_general(flat, dk, outer, preferred_element_type=jnp.float32)
     local_v = lax.dot_general(flat, dv, outer, preferred_element_type=jnp.float32)
-    sum_q, sum_k, sum_v = lax.psum((local_q, local_k, local_v), ("gx", "gy"))
+    shelves_wrap = lambda ax_name, net_axis, chunk: lax.psum(lax.psum(chunk, ax_name), net_axis)
+    sum_q, sum_k, sum_v = shelves_wrap("gy", "gx", (local_q, local_k, local_v))
     mixed = out.reshape(feats.shape)
     return (
         mixed,

time: 446 us -> 690 us (1.55)
  the two profiles are of different devices: /device:TPU:8 before, /device:TPU:104 now
where the time goes in v1:
time: 690 us; the launch traced here: 689 us
  waiting for transfers between devices  303 us (44%)
  blocking collectives  229 us (33%)
  matrix products  66.2 us (10%)
  local copies, waits for them, and re-layouts  43.4 us (6%)
  starting transfers between devices  24.5 us (4%)
  between operations  15 us (2%)
  other arithmetic  7.87 us (1%)
    psum x1, blocking collectives, body(): lax.psum(lax.psum(chunk, ax_name), net_axis)  229 us
    psum x1, waiting for transfers between devices, body(): lax.psum(chunk, ax_name)  213 us
    ppermute x2, waiting for transfers between devices, with_halo(): before = lax.ppermute(last, axis, up)  37.3 us
    ppermute x2, waiting for transfers between devices, with_halo(): after = lax.ppermute(initial, axis, down)  31.8 us
    ppermute x4, waiting for transfers between devices, passed_along(): lax.ppermute(value, axis, [(source, source + steps) for source in range(i...  21.3 us
    dot_general x2, matrix products, one_slot(): jnp.einsum('hqk,qhd->khd', dscore, qh, preferred_element_type=jnp.float32)  17.7 us
    dot_general x2, matrix products, one_slot(): jnp.einsum('hqk,khd->qhd', dscore, kk, preferred_element_type=jnp.float32)  17.1 us
    ppermute x4, starting transfers between devices, passed_along(): lax.ppermute(value, axis, [(source, source + steps) for source in range(i...  14.2 us
  transfers between devices with their start and end apart: 9, of which 6 were waited for; matrix products, arithmetic and copies ran while one was open for 1% of the time, Pallas kernels for 0%

profile of v1, /device:TPU:104, one launch (start us, length us, event | category | flops | bytes accessed | tf_op | source)
XLA Modules:
  0.0 689.0 jit_solution(1554229484138471070)
XLA Ops:
  11.5 3.1 collective-permute-start
  17.5 2.1 collective-permute-start.2
  20.6 3.7 collective-permute-start.3
  28.0 37.0 %collective-permute-done.2 = bf16[3,1,2,128,1024]{4,3,2,1,0:T(8,128)(2,1)} collective-permute-done((bf16[3,1,2,128,1024]{4,3,2,1,0:T(8,128)(2,1)}, bf16[3,1,2,128,1024]{4,3,2,1,0:T(8,128)(2,1)}, u32[]{:S(2)}, u32[]{:S(2)}) %collective-permute-start.2) | collective-permute-done | bytes 1572896 | tf_op jit(solution)/shard_map/ppermute | solution.py:16
  66.8 31.8 %collective-permute-done.3 = bf16[3,1,2,128,1024]{4,3,2,1,0:T(8,128)(2,1)S(1)} collective-permute-done((bf16[3,1,2,128,1024]{4,3,2,1,0:T(8,128)(2,1)}, bf16[3,1,2,128,1024]{4,3,2,1,0:T(8,128)(2,1)S(1)}, u32[]{:S(2)}, u32[]{:S(2)}) %collective-permute-start.3) | collective-permute-done | bytes 1572896 | tf_op jit(solution)/shard_map/ppermute | solution.py:17
  99.5 3.8 gather_fusion
  103.3 81.1 %while.14 = (s32[]{:T(128)}, bf16[2,128,512]{2,1,0:T(8,128)(2,1)}, bf16[2,128,512]{2,1,0:T(8,128)(2,1)}, f32[2,4,128,1024]{3,2,1,0:T(8,128)}, pred[2,128]{1,0:T(...) while((s32[]{:T(128)}, bf16[2,128,512]{2,1,0:T(8,128)(2,1)}, ...), condition=%wide.region_4.5_spmd, body=%wide.region_0.4_spmd.sunk | while | flops 415043072 | bytes 50373096 | solution.py:66
  109.7 3.9 fusion.108
  113.6 2.8 fusion.110
  116.4 8.5 %fusion.109 = bf16[8,64,128]{2,1,0:T(8,128)(2,1)} fusion(bf16[512,8,64]{0,2,1:T(8,128)(2,1)} %bitcast.165, f32[8,128,512]{2,1,0:T(8,128)S(1)} %fusion.107, f32[8,128,512]{2,1,0:T(8,128)} %get-tuple-element.185, f32[8,128]{1,0:T(8,128)S(1)} %copy-done.16), kind=kOutput, calls=%fused_computation.15.clone.1 | convolution fusion | flops 70845952 | bytes 4853760 | tf_op jit(solution)/shard_map/while/body/eval_jaxpr/hqk,khd->qhd/dot_general | solution.py:50
  124.9 8.8 %fusion.111 = f32[512,8,64]{0,2,1:T(8,128)} fusion(bf16[128,8,64]{0,2,1:T(8,128)(2,1)S(1)} %bitcast.180, f32[8,128,512]{2,1,0:T(8,128)S(1)} %fusion.107, f32[8,128,512]{2,1,0:T(8,128)} %get-tuple-element.185, f32[8,128]{1,0:T(8,128)S(1)} %copy-done.16), kind=kOutput, calls=%fused_computation.12.clone.1 | convolution fusion | flops 70780416 | bytes 5378048 | tf_op jit(solution)/shard_map/while/body/eval_jaxpr/hqk,qhd->khd/dot_general | solution.py:52
  150.3 3.9 fusion.108
  154.1 2.8 fusion.110
  156.9 8.5 %fusion.109 = bf16[8,64,128]{2,1,0:T(8,128)(2,1)} fusion(bf16[512,8,64]{0,2,1:T(8,128)(2,1)} %bitcast.165, f32[8,128,512]{2,1,0:T(8,128)S(1)} %fusion.107, f32[8,128,512]{2,1,0:T(8,128)} %get-tuple-element.185, f32[8,128]{1,0:T(8,128)S(1)} %copy-done.16), kind=kOutput, calls=%fused_computation.15.clone.1 | convolution fusion | flops 70845952 | bytes 4853760 | tf_op jit(solution)/shard_map/while/body/eval_jaxpr/hqk,khd->qhd/dot_general | solution.py:50
  165.5 8.8 %fusion.111 = f32[512,8,64]{0,2,1:T(8,128)} fusion(bf16[128,8,64]{0,2,1:T(8,128)(2,1)S(1)} %bitcast.180, f32[8,128,512]{2,1,0:T(8,128)S(1)} %fusion.107, f32[8,128,512]{2,1,0:T(8,128)} %get-tuple-element.185, f32[8,128]{1,0:T(8,128)S(1)} %copy-done.16), kind=kOutput, calls=%fused_computation.12.clone.1 | convolution fusion | flops 70780416 | bytes 5378048 | tf_op jit(solution)/shard_map/while/body/eval_jaxpr/hqk,qhd->khd/dot_general | solution.py:52
  184.5 4.6 copy.40
  189.1 3.6 convolution_convert_fusion
  195.0 4.4 collective-permute-start.5
  199.5 4.0 collective-permute-start.6
  203.5 4.5 collective-permute-start.7
  210.7 8.2 %collective-permute-done.6 = bf16[2,128,1024]{2,1,0:T(8,128)(2,1)S(1)} collective-permute-done((bf16[2,128,1024]{2,1,0:T(8,128)(2,1)S(1)}, bf16[2,128,1024]{2,1,0:T(8,128)(2,1)S(1)}, u32[]{:S(2)}, u32[]{:S(2)}) %collective-permute-start.6) | collective-permute-done | bytes 524320 | tf_op jit(solution)/shard_map/ppermute | solution.py:25
  218.9 13.1 %collective-permute-done.7 = bf16[2,128,1024]{2,1,0:T(8,128)(2,1)S(1)} collective-permute-done((bf16[2,128,1024]{2,1,0:T(8,128)(2,1)S(1)}, bf16[2,128,1024]{2,1,0:T(8,128)(2,1)S(1)}, u32[]{:S(2)}, u32[]{:S(2)}) %collective-permute-start.7) | collective-permute-done | bytes 524320 | tf_op jit(solution)/shard_map/ppermute | solution.py:25
  237.8 212.7 %all-reduce.5.cloned.1.call-done = (f32[512,512]{0,1:T(8,128)}, f32[512,512]{0,1:T(8,128)}, f32[512,512]{0,1:T(8,128)}) async-done(((f32[512,512]{0,1:T(8,128)}, f32[512,512]{0,1:T(8,128)}, f32[512,512]{0,1:T(8,128)}), (f32[512,512]{0,1:T(8,128)}, f32[512,512]{0,1:T(8,128)}, f32[512,512]{0,1:T(8,128)})) %all-reduce.5.cloned.1.call-update) | async-done | bytes 3145744 | tf_op jit(solution)/shard_map/psum | solution.py:125
  450.4 228.7 %all-reduce.6 = (bf16[512,512]{0,1:T(8,128)(2,1)S(1)}, bf16[512,512]{0,1:T(8,128)(2,1)S(1)}, bf16[512,512]{0,1:T(8,128)(2,1)S(1)}) all-reduce(f32[512,512]{0,1:T(8,128)} %get-tuple-element.106, f32[512,512]{0,1:T(8,128)} %get-tuple-element.107, f32[512,512]{0,1:T(8,128)} %get-tuple-element.108), channel_id=1, replica_groups=mesh['gx'=32,'gy'=16] {'gx'}, use_global_device_ids=true, to_apply=%region_6.7 | all-reduce | flops 786432 | bytes 4718592 | tf_op jit(solution)/shard_map/psum | solution.py:125
  (138 shorter events, 60.4 us)
Async XLA Ops:
  7.2 18.1 %copy-start = (bf16[512,512]{1,0:T(8,128)(2,1)S(1)}, bf16[512,512]{1,0:T(8,128)(2,1)}, u32[]{:S(2)}) copy-start(bf16[512,512]{1,0:T(8,128)(2,1)} %param.12) | copy-start | bytes 1572868
  7.2 8.1 %copy-start.13 = (s32[1,1,2]{2,1,0:T(1,128)S(1)}, s32[1,1,2]{2,1,0:T(1,128)}, u32[]{:S(2)}) copy-start(s32[1,1,2]{2,1,0:T(1,128)} %param.17) | copy-start | bytes 28
  7.2 8.2 %copy-start.11 = (s32[1,1,2,3]{3,2,1,0:T(2,128)S(1)}, s32[1,1,2,3]{3,2,1,0:T(2,128)}, u32[]{:S(2)}) copy-start(s32[1,1,2,3]{3,2,1,0:T(2,128)} %param.18) | copy-start | bytes 76
  7.2 8.3 %copy-start.12 = (s32[1,1,2,3]{3,2,1,0:T(2,128)S(1)}, s32[1,1,2,3]{3,2,1,0:T(2,128)}, u32[]{:S(2)}) copy-start(s32[1,1,2,3]{3,2,1,0:T(2,128)} %param.19) | copy-start | bytes 76
  7.2 443.2 %all-reduce.5.cloned.1.call-start = ((), (), s32[]{:S(2)}) async-start(), calls=%async_computation | async-start | bytes 6291456 | tf_op jit(solution)/shard_map/psum | solution.py:125
  10.2 9.5 %copy-start.10 = (bf16[1,1,2,128,512]{4,3,2,1,0:T(8,128)(2,1)S(1)}, bf16[1,1,2,128,512]{4,3,2,1,0:T(8,128)(2,1)}, u32[]{:S(2)}) copy-start(bf16[1,1,2,128,512]{4,3,2,1,0:T(8,128)(2,1)} %param.15) | copy-start | bytes 786436
  10.2 5.5 collective-permute-start.1
  11.5 4.6 collective-permute-start
  15.7 9.6 %copy-start.1 = (bf16[1,1,2,128,512]{4,3,2,1,0:T(8,128)(2,1)S(1)}, bf16[1,1,2,128,512]{4,3,2,1,0:T(8,128)(2,1)}, u32[]{:S(2)}) copy-start(bf16[1,1,2,128,512]{4,3,2,1,0:T(8,128)(2,1)} %param.11) | copy-start | bytes 786436
  17.5 47.5 %collective-permute-start.2 = (bf16[3,1,2,128,1024]{4,3,2,1,0:T(8,128)(2,1)}, bf16[3,1,2,128,1024]{4,3,2,1,0:T(8,128)(2,1)}, u32[]{:S(2)}, u32[]{:S(2)}) collective-permute-start(bf16[3,1,2,128,1024]{4,3,2,1,0:T(8,128)(2,1)} %pad_maximum_fusion), channel_id=1, source_target_pairs={{0,1},{1,2},{2,3},{3,4},{4,5},{5,6},{6,7},{7,8},{8,9},{9,10},{10,1... | collective-permute-start | bytes 4718600 | tf_op jit(solution)/shard_map/ppermute | solution.py:16
  20.6 78.0 %collective-permute-start.3 = (bf16[3,1,2,128,1024]{4,3,2,1,0:T(8,128)(2,1)}, bf16[3,1,2,128,1024]{4,3,2,1,0:T(8,128)(2,1)S(1)}, u32[]{:S(2)}, u32[]{:S(2)}) collective-permute-start(bf16[3,1,2,128,1024]{4,3,2,1,0:T(8,128)(2,1)} %pad_maximum_fusion), channel_id=1, source_target_pairs={{1,0},{2,1},{3,2},{4,3},{5,4},{6,5},{7,6},{8,7},{9,8},{10,9},{11,1... | collective-permute-start | bytes 4718600 | tf_op jit(solution)/shard_map/ppermute | solution.py:17
  113.6 2.8 copy-start.16
  116.4 8.5 %copy-start.3 = (bf16[1,128,512]{1,2,0:T(8,128)(2,1)S(1)}, bf16[1,128,512]{1,2,0:T(8,128)(2,1)}, u32[]{:S(2)}) copy-start(bf16[1,128,512]{1,2,0:T(8,128)(2,1)} %copy.62) | copy-start | bytes 393220 | tf_op jit(solution)/shard_map/while
  139.5 2.1 copy-start.2
  139.5 2.3 copy-start.7
  154.1 2.8 copy-start.16
  156.9 8.5 %copy-start.3 = (bf16[1,128,512]{1,2,0:T(8,128)(2,1)S(1)}, bf16[1,128,512]{1,2,0:T(8,128)(2,1)}, u32[]{:S(2)}) copy-start(bf16[1,128,512]{1,2,0:T(8,128)(2,1)} %copy.62) | copy-start | bytes 393220 | tf_op jit(solution)/shard_map/while
  180.0 2.1 copy-start.2
  180.0 2.3 copy-start.7
  194.5 14.8 %copy-start.9 = (bf16[2,128,512]{2,1,0:T(8,128)(2,1)S(1)}, bf16[2,128,512]{2,1,0:T(8,128)(2,1)}, u32[]{:S(2)}) copy-start(bf16[2,128,512]{2,1,0:T(8,128)(2,1)} %get-tuple-element.55) | copy-start | bytes 786436
  195.0 15.6 %collective-permute-start.5 = (bf16[2,128,1024]{2,1,0:T(8,128)(2,1)S(1)}, bf16[2,128,1024]{2,1,0:T(8,128)(2,1)S(1)}, u32[]{:S(2)}, u32[]{:S(2)}) collective-permute-start(bf16[2,128,1024]{2,1,0:T(8,128)(2,1)S(1)} %bitcast.195), channel_id=1, source_target_pairs={{0,16},{16,32},{32,48},{48,64},{64,80},{80,96},{96,112},{112,128},... | collective-permute-start | bytes 1572872 | tf_op jit(solution)/shard_map/ppermute | solution.py:25
  199.5 19.4 %collective-permute-start.6 = (bf16[2,128,1024]{2,1,0:T(8,128)(2,1)S(1)}, bf16[2,128,1024]{2,1,0:T(8,128)(2,1)S(1)}, u32[]{:S(2)}, u32[]{:S(2)}) collective-permute-start(bf16[2,128,1024]{2,1,0:T(8,128)(2,1)S(1)} %bitcast.194), channel_id=1, source_target_pairs={{1,0},{2,1},{3,2},{4,3},{5,4},{6,5},{7,6},{8,7},{9,8},{10,9},{11,1... | collective-permute-start | bytes 1572872 | tf_op jit(solution)/shard_map/ppermute | solution.py:25
  203.5 28.5 %collective-permute-start.7 = (bf16[2,128,1024]{2,1,0:T(8,128)(2,1)S(1)}, bf16[2,128,1024]{2,1,0:T(8,128)(2,1)S(1)}, u32[]{:S(2)}, u32[]{:S(2)}) collective-permute-start(bf16[2,128,1024]{2,1,0:T(8,128)(2,1)S(1)} %bitcast.193), channel_id=1, source_target_pairs={{0,1},{1,2},{2,3},{3,4},{4,5},{5,6},{6,7},{7,8},{8,9},{9,10},{10,1... | collective-permute-start | bytes 1572872 | tf_op jit(solution)/shard_map/ppermute | solution.py:25
  208.0 24.0 %collective-permute-start.4 = (bf16[2,128,1024]{2,1,0:T(8,128)(2,1)S(1)}, bf16[2,128,1024]{2,1,0:T(8,128)(2,1)S(1)}, u32[]{:S(2)}, u32[]{:S(2)}) collective-permute-start(bf16[2,128,1024]{2,1,0:T(8,128)(2,1)S(1)} %bitcast.192), channel_id=1, source_target_pairs={{16,0},{32,16},{48,32},{64,48},{80,64},{96,80},{112,96},{128,112},... | collective-permute-start | bytes 1572872 | tf_op jit(solution)/shard_map/ppermute | solution.py:25
  (10 other events, 13.4 us)
Sparse Core Ops, SparseCore 0:
  235.5 214.8 all-reduce.4
